TPU v7x, 512 devices: a whole 4x8x8 slice. The times are simulated.
512 devices in a mesh: col: 64 (over y, z_lo, core), row: 8 (over x, z_hi).
Axes of the slice: x: 4, y: 8, z: 8 (z_hi: 2, z_lo: 4; z = z_hi * 4 + z_lo), core: 2. Of those that a mesh axis runs over, the one named last changes fastest.
Arguments:
- field: bfloat16 [128, 1024, 128], P('row', 'col'), may hold values from -6 to 6
- cotangent: bfloat16 [128, 1024, 128], P('row', 'col'), may hold values from -6 to 6
- w_first: bfloat16 [3, 3, 128, 128], replicated, may hold values from -0.1875 to 0.1875
- w_down: bfloat16 [3, 3, 128, 256], replicated, may hold values from -0.1875 to 0.1875
- w_up: bfloat16 [2, 2, 256, 128], replicated, may hold values from -0.375 to 0.375
- offsets: int32 [8, 64, 2], replicated, may hold values from -8 to 8
- blend_table: int32 [32, 32], replicated, may hold values from 1 to 16
Outputs:
- blended: bfloat16 [128, 1024, 128], P('row', 'col')
- field_grad: float32 [128, 1024, 128], P('row', 'col')
- grad_first: float32 [3, 3, 128, 128], replicated
- grad_down: float32 [3, 3, 128, 256], replicated
- grad_up: float32 [2, 2, 256, 128], replicated
Inputs may be any that keep to these rules, and one draw needn't show every extreme that they name: `offsets`: A patch's first cell lies 8 cells minus its offset before its tile's first cell on each axis.
All inputs are finite; a program needn't handle non-finite values.
Results may differ from a plain program's by a relative error of at most 0.015.
Values may be sent and summed in bfloat16 or wider, within the bound.
No kernel may reach another device: no remote copies, remote signals or barrier semaphores. Data moves between devices by JAX's collectives and lax.ppermute only.
A program may use at most 64 MiB of HBM per device.

v0:
```python
import math
import jax
import jax.numpy as jnp
from jax import lax
from jax.sharding import PartitionSpec as P

MARGIN = 8


def passed_along(block, axis, distance):
    devices = range(lax.axis_size(axis))
    route = [(i - distance, i) for i in devices if i - distance in devices]
    return lax.ppermute(block, axis, route)


def extended(x, sides, width):
    for axis, dim in sides:
        size, length = (lax.axis_size(axis), x.shape[dim])
        up = [(i, (i + 1) % size) for i in range(size - 1)]
        down = [(j, i) for i, j in up]
        last = lax.slice_in_dim(x, length - width, length, axis=dim)
        leading = lax.slice_in_dim(x, 0, width, axis=dim)
        before = lax.ppermute(last, axis, up)
        after = lax.ppermute(leading, axis, down)
        x = jnp.concatenate([before, x, after], axis=dim)
    return x


def conv_same(inputs, kernel):
    rows, cols, chans = inputs.shape
    padded = jnp.pad(inputs, ((1, 1), (1, 1), (0, 0)))
    total = jnp.zeros((rows * cols, kernel.shape[3]), jnp.float32)
    for row_tap in range(3):
        for col_tap in range(3):
            window = padded[row_tap : row_tap + rows, col_tap : col_tap + cols].reshape(
                rows * cols, chans
            )
            total = total + jnp.dot(
                window, kernel[row_tap, col_tap], preferred_element_type=jnp.float32
            )
    return total.reshape(rows, cols, kernel.shape[3])


def conv_down(inputs, kernel):
    rows, cols, chans = inputs.shape
    padded = jnp.pad(inputs, ((1, 1), (1, 1), (0, 0)))
    half_r = rows // 2
    half_c = cols // 2
    total = jnp.zeros((half_r * half_c, kernel.shape[3]), jnp.float32)
    for row_tap in range(3):
        for col_tap in range(3):
            window = padded[row_tap : row_tap + rows : 2, col_tap : col_tap + cols : 2].reshape(
                half_r * half_c, chans
            )
            total = total + jnp.dot(
                window, kernel[row_tap, col_tap], preferred_element_type=jnp.float32
            )
    return total.reshape(half_r, half_c, kernel.shape[3])


def conv_up(inputs, kernel):
    rows, cols, chans = inputs.shape
    flat = inputs.reshape(rows * cols, chans)
    lines = []
    for row_tap in range(2):
        pieces = []
        for col_tap in range(2):
            pieces.append(
                jnp.dot(flat, kernel[row_tap, col_tap], preferred_element_type=jnp.float32).reshape(
                    rows, cols, kernel.shape[3]
                )
            )
        lines.append(jnp.stack(pieces, axis=2))
    return jnp.stack(lines, axis=1).reshape(2 * rows, 2 * cols, kernel.shape[3])


def patch_net(patch, w_first, w_down, w_up):
    hidden = jax.nn.silu(conv_same(patch, w_first)).astype(jnp.bfloat16)
    lower = jax.nn.silu(conv_down(hidden, w_down)).astype(jnp.bfloat16)
    return hidden.astype(jnp.float32) + conv_up(lower, w_up)


def return_margins(canvas, tile_h, tile_w, edge):
    summed = canvas
    for heading in (1, -1):
        strip = canvas[tile_h + edge :] if heading == 1 else canvas[:edge]
        arrived = passed_along(strip.astype(jnp.bfloat16), "row", heading).astype(strip.dtype)
        if heading == 1:
            summed = summed.at[edge : 2 * edge].add(arrived)
        else:
            summed = summed.at[tile_h : tile_h + edge].add(arrived)
    middle = summed[edge : tile_h + edge]
    result = middle
    for heading in (1, -1):
        strip = middle[:, tile_w + edge :] if heading == 1 else middle[:, :edge]
        arrived = passed_along(strip.astype(jnp.bfloat16), "col", heading).astype(strip.dtype)
        if heading == 1:
            result = result.at[:, edge : 2 * edge].add(arrived)
        else:
            result = result.at[:, tile_w : tile_w + edge].add(arrived)
    return result[:, edge : tile_w + edge]


def weight_total(offsets, table_f, row_at, col_at, rows_n, cols_n, tile_h, tile_w, lead, reach):
    patch_h, patch_w = table_f.shape
    total = jnp.zeros((tile_h + 2 * lead, tile_w + 2 * lead), jnp.float32)
    for row_step in range(-reach, reach + 1):
        for col_step in range(-reach, reach + 1):
            near_row = row_at + row_step
            near_col = col_at + col_step
            inside = (
                (near_row >= 0) & (near_row < rows_n) & (near_col >= 0) & (near_col < cols_n)
            ).astype(jnp.float32)
            shift_pair = offsets[
                jnp.clip(near_row, 0, rows_n - 1), jnp.clip(near_col, 0, cols_n - 1)
            ]
            top = row_step * tile_h - MARGIN + shift_pair[0] + lead
            left = col_step * tile_w - MARGIN + shift_pair[1] + lead
            pick_rows = (
                jnp.arange(tile_h + 2 * lead)[:, None] - top == jnp.arange(patch_h)[None, :]
            ).astype(jnp.float32)
            pick_cols = (
                jnp.arange(tile_w + 2 * lead)[:, None] - left == jnp.arange(patch_w)[None, :]
            ).astype(jnp.float32)
            placed = jnp.dot(
                jnp.dot(pick_rows, table_f, precision=lax.Precision.HIGHEST),
                pick_cols.T,
                precision=lax.Precision.HIGHEST,
            )
            total = total + inside * placed
    return total


def per_device(field, cotangent, w_first, w_down, w_up, offsets, blend_table):
    tile_h, tile_w, chans = field.shape
    patch_h, patch_w = blend_table.shape
    edge = 2 * MARGIN
    rows_n = lax.axis_size("row")
    cols_n = lax.axis_size("col")
    row_at = lax.axis_index("row")
    col_at = lax.axis_index("col")
    table_f = blend_table.astype(jnp.float32)
    grown = extended(field, (("row", 0), ("col", 1)), edge)
    own_shift = offsets[row_at, col_at]
    start_r = MARGIN + own_shift[0]
    start_c = MARGIN + own_shift[1]
    zero = jnp.int32(0)
    patch = lax.dynamic_slice(grown, (start_r, start_c, zero), (patch_h, patch_w, chans))
    out_patch, back = jax.vjp(patch_net, patch, w_first, w_down, w_up)
    empty = jnp.zeros((tile_h + 2 * edge, tile_w + 2 * edge, chans), jnp.float32)
    canvas = lax.dynamic_update_slice(
        empty, table_f[:, :, None] * out_patch, (start_r, start_c, zero)
    )
    numer = return_margins(canvas, tile_h, tile_w, edge)
    weight_sum = weight_total(
        offsets, table_f, row_at, col_at, rows_n, cols_n, tile_h, tile_w, 0, 1
    )
    ratio = cotangent.astype(jnp.float32) / weight_sum[:, :, None]
    ratio_grown = extended(ratio.astype(jnp.bfloat16), (("row", 0), ("col", 1)), edge).astype(
        ratio.dtype
    )
    blended = (numer / weight_sum[:, :, None]).astype(jnp.bfloat16)
    out_grad = table_f[:, :, None] * lax.dynamic_slice(
        ratio_grown, (start_r, start_c, zero), (patch_h, patch_w, chans)
    )
    d_patch, d_first, d_down, d_up = back(out_grad)
    d_canvas = lax.dynamic_update_slice(
        empty, d_patch.astype(jnp.float32), (start_r, start_c, zero)
    )
    field_grad = return_margins(d_canvas, tile_h, tile_w, edge)
    g_first, g_down, g_up = lax.psum(
        (d_first.astype(jnp.float32), d_down.astype(jnp.float32), d_up.astype(jnp.float32)),
        ("col", "row"),
    )
    scale = 1.0 / math.sqrt(tile_h * rows_n * tile_w * cols_n)
    return (blended, field_grad, g_first * scale, g_down * scale, g_up * scale)


def solution(mesh):
    return jax.shard_map(
        per_device,
        mesh=mesh,
        in_specs=(P("row", "col", None), P("row", "col", None), P(), P(), P(), P(), P()),
        out_specs=(P("row", "col", None), P("row", "col", None), P(), P(), P()),
        check_vma=False,
    )
```

profile of v0, /device:TPU:17, one launch (start us, length us, event | category | flops | bytes accessed | tf_op | source)
XLA Modules:
  0.0 498.5 jit_solution(4310469566527345241)
XLA Ops:
  7.2 10.6 %collective-permute-start = (bf16[16,16,128]{2,1,0:T(8,128)(2,1)}, bf16[16,16,128]{2,1,0:T(8,128)(2,1)S(1)}, u32[]{:S(2)}, u32[]{:S(2)}) collective-permute-start(bf16[16,16,128]{2,1,0:T(8,128)(2,1)} %param.23), channel_id=1, source_target_pairs={{0,1},{1,2},{2,3},{3,4},{4,5},{5,6},{6,7},{8,9},{9,10},{10,11},{11... | collective-permute-start | bytes 196616 | tf_op jit(solution)/shard_map/ppermute | solution.py:23
  17.9 1.3 collective-permute-start.1
  45.4 3.9 collective-permute-start.2
  49.3 1.9 collective-permute-start.3
  51.4 8.1 %collective-permute-start.8 = (bf16[16,16,128]{2,1,0:T(8,128)(2,1)S(1)}, bf16[16,16,128]{2,1,0:T(8,128)(2,1)S(1)}, u32[]{:S(2)}, u32[]{:S(2)}) collective-permute-start(bf16[16,16,128]{2,1,0:T(8,128)(2,1)S(1)} %divide_convert_fusion), channel_id=1, source_target_pairs={{0,1},{1,2},{2,3},{3,4},{4,5},{5,6},{6,7},{8,9},{9,10},{10,11},{11... | collective-permute-start | bytes 196616 | tf_op jit(solution)/shard_map/ppermute | solution.py:23
  59.5 1.3 collective-permute-start.9
  63.4 5.0 %collective-permute-done.9 = bf16[16,16,128]{2,1,0:T(8,128)(2,1)S(1)} collective-permute-done((bf16[16,16,128]{2,1,0:T(8,128)(2,1)S(1)}, bf16[16,16,128]{2,1,0:T(8,128)(2,1)S(1)}, u32[]{:S(2)}, u32[]{:S(2)}) %collective-permute-start.9) | collective-permute-done | bytes 65568 | tf_op jit(solution)/shard_map/ppermute | solution.py:24
  69.2 5.7 %collective-permute-start.10 = (bf16[48,16,128]{2,1,0:T(8,128)(2,1)}, bf16[48,16,128]{2,1,0:T(8,128)(2,1)}, u32[]{:S(2)}, u32[]{:S(2)}) collective-permute-start(bf16[48,16,128]{2,1,0:T(8,128)(2,1)} %pad_maximum_fusion.1), channel_id=1, source_target_pairs={{0,8},{8,16},{16,24},{24,32},{32,40},{40,48},{48,56},{56,64},{64,7... | collective-permute-start | bytes 589832 | tf_op jit(solution)/shard_map/ppermute | solution.py:23
  74.9 2.8 collective-permute-start.11
  88.6 2.3 convert_multiply_fusion.2
  107.4 5.6 %pad.156 = bf16[34,34,128]{2,1,0:T(8,128)(2,1)S(1)} pad(bf16[16,16,128]{2,1,0:T(8,128)(2,1)} %bitcast.505, bf16[]{:T(256)} %constant.241.clone.1), padding=2_1_1x0_3_1x0_0_0 | pad | bytes 361474 | tf_op jit(solution)/shard_map/transpose(jvp())/pad | solution.py:52
  113.0 8.5 %pad.345 = bf16[33,33,128]{2,1,0:T(8,128)(2,1)} pad(bf16[16,16,128]{2,1,0:T(8,128)(2,1)} %bitcast.504, bf16[]{:T(256)} %constant.241.clone.1), padding=0_2_1x0_2_1x0_0_0 | pad | bytes 344322
  121.5 8.5 %pad.348 = bf16[32,33,128]{2,1,0:T(8,128)(2,1)} pad(bf16[16,16,128]{2,1,0:T(8,128)(2,1)} %bitcast.511, bf16[]{:T(256)} %constant.241.clone.1), padding=0_1_1x0_2_1x0_0_0 | pad | bytes 335874
  130.0 8.4 %pad.346 = bf16[33,32,128]{2,1,0:T(8,128)(2,1)} pad(bf16[16,16,128]{2,1,0:T(8,128)(2,1)} %bitcast.510, bf16[]{:T(256)} %constant.241.clone.1), padding=0_2_1x0_1_1x0_0_0 | pad | bytes 335874
  138.4 8.4 %pad.347 = bf16[33,32,128]{2,1,0:T(8,128)(2,1)} pad(bf16[16,16,128]{2,1,0:T(8,128)(2,1)} %bitcast.509, bf16[]{:T(256)} %constant.241.clone.1), padding=0_2_1x1_0_1x0_0_0 | pad | bytes 335874
  146.8 8.4 %pad.214 = bf16[32,32,128]{2,1,0:T(8,128)(2,1)} pad(bf16[16,16,128]{2,1,0:T(8,128)(2,1)} %bitcast.503, bf16[]{:T(256)} %constant.241.clone.1), padding=0_1_1x1_0_1x0_0_0 | pad | bytes 327682 | tf_op jit(solution)/shard_map/transpose(jvp(jit(_pad)))/pad | solution.py:46
  155.2 5.6 %pad.215 = bf16[32,32,128]{2,1,0:T(8,128)(2,1)} pad(bf16[16,16,128]{2,1,0:T(8,128)(2,1)S(1)} %bitcast.502, bf16[]{:T(256)} %constant.241.clone.1), padding=0_1_1x0_1_1x0_0_0 | pad | bytes 327682 | tf_op jit(solution)/shard_map/transpose(jvp(jit(_pad)))/pad | solution.py:46
  162.0 1.7 fusion.52
  172.8 1.3 dynamic_update_slice.7
  174.9 4.2 collective-permute-start.12
  179.1 1.3 collective-permute-start.13
  180.4 1.3 dynamic_update_slice.6
  182.7 8.6 %collective-permute-start.4 = (bf16[16,48,128]{2,1,0:T(8,128)(2,1)}, bf16[16,48,128]{2,1,0:T(8,128)(2,1)}, u32[]{:S(2)}, u32[]{:S(2)}) collective-permute-start(bf16[16,48,128]{2,1,0:T(8,128)(2,1)} %get-tuple-element.110), channel_id=1, source_target_pairs={{0,1},{1,2},{2,3},{3,4},{4,5},{5,6},{6,7},{8,9},{9,10},{10,11},{11... | collective-permute-start | bytes 589832 | tf_op jit(solution)/shard_map/ppermute | solution.py:13
  191.2 1.3 collective-permute-start.5
  195.8 11.9 %collective-permute-done.5 = bf16[16,48,128]{2,1,0:T(8,128)(2,1)} collective-permute-done((bf16[16,48,128]{2,1,0:T(8,128)(2,1)S(1)}, bf16[16,48,128]{2,1,0:T(8,128)(2,1)}, u32[]{:S(2)}, u32[]{:S(2)}) %collective-permute-start.5) | collective-permute-done | bytes 196640 | tf_op jit(solution)/shard_map/ppermute | solution.py:13
  208.7 12.5 %collective-permute-start.6 = (bf16[16,16,128]{2,1,0:T(8,128)(2,1)S(1)}, bf16[16,16,128]{2,1,0:T(8,128)(2,1)S(1)}, u32[]{:S(2)}, u32[]{:S(2)}) collective-permute-start(bf16[16,16,128]{2,1,0:T(8,128)(2,1)S(1)} %get-tuple-element.128), channel_id=1, source_target_pairs={{0,8},{8,16},{16,24},{24,32},{32,40},{40,48},{48,56},{56,64},{64,7... | collective-permute-start | bytes 196616 | tf_op jit(solution)/shard_map/ppermute | solution.py:13
  221.3 1.9 collective-permute-start.7
  224.3 3.6 collective-permute-start.14
  228.0 1.9 collective-permute-start.15
  230.7 3.3 collective-permute-done.15
  234.7 252.5 %all-reduce.45.cloned.1.call-done = (f32[3,3,128,128]{3,2,1,0:T(8,128)}, f32[3,3,128,256]{3,2,1,0:T(8,128)}, f32[2,2,256,128]{3,2,1,0:T(8,128)}) async-done(((f32[3,3,128,128]{3,2,1,0:T(8,128)}, f32[3,3,128,256]{3,2,1,0:T(8,128)}, f32[2,2,256,128]{3,2,1,0:T(8,128)}), (f32[3,3,128,128]{3,2,1,0:T(8,128)}, f32[3,3,128,256]{3,2,1,0:T(8,128)}, f32[2,2,256,128]{3,2,1,0:T(8,128)})) %all-reduce.45.cloned.1.call-update) | async-done | bytes 2293776 | tf_op jit(solution)/shard_map/psum | solution.py:171
  487.1 2.4 broadcast_multiply_fusion
  (260 shorter events, 62.5 us)
Async XLA Ops:
  7.2 38.1 %copy-start.35 = (bf16[16,16,128]{2,1,0:T(8,128)(2,1)S(1)}, bf16[16,16,128]{2,1,0:T(8,128)(2,1)}, u32[]{:S(2)}) copy-start(bf16[16,16,128]{2,1,0:T(8,128)(2,1)} %param.23) | copy-start | bytes 196612
  7.2 56.2 %copy-start.43 = (s32[32,32]{1,0:T(8,128)S(1)}, s32[32,32]{1,0:T(8,128)}, u32[]{:S(2)}) copy-start(s32[32,32]{1,0:T(8,128)} %param.29) | copy-start | bytes 12292
  7.2 44.1 %copy-start.36 = (bf16[16,16,128]{2,1,0:T(8,128)(2,1)S(1)}, bf16[16,16,128]{2,1,0:T(8,128)(2,1)}, u32[]{:S(2)}) copy-start(bf16[16,16,128]{2,1,0:T(8,128)(2,1)} %param.24) | copy-start | bytes 196612
  7.2 479.9 %all-reduce.45.cloned.1.call-start = ((), (), s32[]{:S(2)}) async-start(), calls=%async_computation | async-start | bytes 4587520 | tf_op jit(solution)/shard_map/psum | solution.py:171
  7.2 38.0 %collective-permute-start = (bf16[16,16,128]{2,1,0:T(8,128)(2,1)}, bf16[16,16,128]{2,1,0:T(8,128)(2,1)S(1)}, u32[]{:S(2)}, u32[]{:S(2)}) collective-permute-start(bf16[16,16,128]{2,1,0:T(8,128)(2,1)} %param.23), channel_id=1, source_target_pairs={{0,1},{1,2},{2,3},{3,4},{4,5},{5,6},{6,7},{8,9},{9,10},{10,11},{11... | collective-permute-start | bytes 196616 | tf_op jit(solution)/shard_map/ppermute | solution.py:23
  17.9 27.5 %collective-permute-start.1 = (bf16[16,16,128]{2,1,0:T(8,128)(2,1)}, bf16[16,16,128]{2,1,0:T(8,128)(2,1)S(1)}, u32[]{:S(2)}, u32[]{:S(2)}) collective-permute-start(bf16[16,16,128]{2,1,0:T(8,128)(2,1)} %param.23), channel_id=1, source_target_pairs={{1,0},{2,1},{3,2},{4,3},{5,4},{6,5},{7,6},{9,8},{10,9},{11,10},{12... | collective-permute-start | bytes 196616 | tf_op jit(solution)/shard_map/ppermute | solution.py:24
  45.4 32.4 %collective-permute-start.2 = (bf16[48,16,128]{2,1,0:T(8,128)(2,1)S(1)}, bf16[48,16,128]{2,1,0:T(8,128)(2,1)S(1)}, u32[]{:S(2)}, u32[]{:S(2)}) collective-permute-start(bf16[48,16,128]{2,1,0:T(8,128)(2,1)S(1)} %constant_dynamic-update-slice_fusion), channel_id=1, source_target_pairs={{0,8},{8,16},{16,24},{24,32},{32,40},{40,48},{48,56},{56,64},{64,7... | collective-permute-start | bytes 589832 | tf_op jit(solution)/shard_map/ppermute | solution.py:23
  49.3 28.4 %collective-permute-start.3 = (bf16[48,16,128]{2,1,0:T(8,128)(2,1)S(1)}, bf16[48,16,128]{2,1,0:T(8,128)(2,1)S(1)}, u32[]{:S(2)}, u32[]{:S(2)}) collective-permute-start(bf16[48,16,128]{2,1,0:T(8,128)(2,1)S(1)} %constant_dynamic-update-slice_fusion), channel_id=1, source_target_pairs={{8,0},{16,8},{24,16},{32,24},{40,32},{48,40},{56,48},{64,56},{72,6... | collective-permute-start | bytes 589832 | tf_op jit(solution)/shard_map/ppermute | solution.py:24
  51.4 12.0 %collective-permute-start.8 = (bf16[16,16,128]{2,1,0:T(8,128)(2,1)S(1)}, bf16[16,16,128]{2,1,0:T(8,128)(2,1)S(1)}, u32[]{:S(2)}, u32[]{:S(2)}) collective-permute-start(bf16[16,16,128]{2,1,0:T(8,128)(2,1)S(1)} %divide_convert_fusion), channel_id=1, source_target_pairs={{0,1},{1,2},{2,3},{3,4},{4,5},{5,6},{6,7},{8,9},{9,10},{10,11},{11... | collective-permute-start | bytes 196616 | tf_op jit(solution)/shard_map/ppermute | solution.py:23
  59.5 9.0 %collective-permute-start.9 = (bf16[16,16,128]{2,1,0:T(8,128)(2,1)S(1)}, bf16[16,16,128]{2,1,0:T(8,128)(2,1)S(1)}, u32[]{:S(2)}, u32[]{:S(2)}) collective-permute-start(bf16[16,16,128]{2,1,0:T(8,128)(2,1)S(1)} %divide_convert_fusion), channel_id=1, source_target_pairs={{1,0},{2,1},{3,2},{4,3},{5,4},{6,5},{7,6},{9,8},{10,9},{11,10},{12... | collective-permute-start | bytes 196616 | tf_op jit(solution)/shard_map/ppermute | solution.py:24
  63.4 14.9 %copy-start.29 = (bf16[16,16,128]{2,1,0:T(8,128)(2,1)}, bf16[16,16,128]{2,1,0:T(8,128)(2,1)S(1)}, u32[]{:S(2)}) copy-start(bf16[16,16,128]{2,1,0:T(8,128)(2,1)S(1)} %collective-permute-done.8) | copy-start | bytes 196612
  69.2 19.0 %collective-permute-start.10 = (bf16[48,16,128]{2,1,0:T(8,128)(2,1)}, bf16[48,16,128]{2,1,0:T(8,128)(2,1)}, u32[]{:S(2)}, u32[]{:S(2)}) collective-permute-start(bf16[48,16,128]{2,1,0:T(8,128)(2,1)} %pad_maximum_fusion.1), channel_id=1, source_target_pairs={{0,8},{8,16},{16,24},{24,32},{32,40},{40,48},{48,56},{56,64},{64,7... | collective-permute-start | bytes 589832 | tf_op jit(solution)/shard_map/ppermute | solution.py:23
  74.9 13.3 %collective-permute-start.11 = (bf16[48,16,128]{2,1,0:T(8,128)(2,1)}, bf16[48,16,128]{2,1,0:T(8,128)(2,1)}, u32[]{:S(2)}, u32[]{:S(2)}) collective-permute-start(bf16[48,16,128]{2,1,0:T(8,128)(2,1)} %pad_maximum_fusion.1), channel_id=1, source_target_pairs={{8,0},{16,8},{24,16},{32,24},{40,32},{48,40},{56,48},{64,56},{72,6... | collective-permute-start | bytes 589832 | tf_op jit(solution)/shard_map/ppermute | solution.py:24
  174.9 48.3 %collective-permute-start.12 = (bf16[16,48,128]{2,1,0:T(8,128)(2,1)}, bf16[16,48,128]{2,1,0:T(8,128)(2,1)}, u32[]{:S(2)}, u32[]{:S(2)}) collective-permute-start(bf16[16,48,128]{2,1,0:T(8,128)(2,1)} %get-tuple-element.108), channel_id=1, source_target_pairs={{0,1},{1,2},{2,3},{3,4},{4,5},{5,6},{6,7},{8,9},{9,10},{10,11},{11... | collective-permute-start | bytes 589832 | tf_op jit(solution)/shard_map/ppermute | solution.py:13
  179.1 44.1 %collective-permute-start.13 = (bf16[16,48,128]{2,1,0:T(8,128)(2,1)S(1)}, bf16[16,48,128]{2,1,0:T(8,128)(2,1)}, u32[]{:S(2)}, u32[]{:S(2)}) collective-permute-start(bf16[16,48,128]{2,1,0:T(8,128)(2,1)S(1)} %get-tuple-element.109), channel_id=1, source_target_pairs={{1,0},{2,1},{3,2},{4,3},{5,4},{6,5},{7,6},{9,8},{10,9},{11,10},{12... | collective-permute-start | bytes 589832 | tf_op jit(solution)/shard_map/ppermute | solution.py:13
  181.8 11.5 %copy-start.37 = (bf16[1,1,128,128]{3,2,1,0:T(8,128)(2,1)S(1)}, bf16[1,1,128,128]{3,2,1,0:T(8,128)(2,1)}, u32[]{:S(2)}) copy-start(bf16[1,1,128,128]{3,2,1,0:T(8,128)(2,1)} %fusion.38) | copy-start | bytes 98308
  181.9 11.5 %copy-start.38 = (bf16[1,1,128,128]{3,2,1,0:T(8,128)(2,1)S(1)}, bf16[1,1,128,128]{3,2,1,0:T(8,128)(2,1)}, u32[]{:S(2)}) copy-start(bf16[1,1,128,128]{3,2,1,0:T(8,128)(2,1)} %fusion.39) | copy-start | bytes 98308
  181.9 11.5 %copy-start.39 = (bf16[1,1,128,128]{3,2,1,0:T(8,128)(2,1)S(1)}, bf16[1,1,128,128]{3,2,1,0:T(8,128)(2,1)}, u32[]{:S(2)}) copy-start(bf16[1,1,128,128]{3,2,1,0:T(8,128)(2,1)} %fusion.40) | copy-start | bytes 98308
  181.9 11.5 %copy-start.40 = (bf16[1,1,128,128]{3,2,1,0:T(8,128)(2,1)S(1)}, bf16[1,1,128,128]{3,2,1,0:T(8,128)(2,1)}, u32[]{:S(2)}) copy-start(bf16[1,1,128,128]{3,2,1,0:T(8,128)(2,1)} %fusion.41) | copy-start | bytes 98308
  181.9 12.4 %copy-start.17 = (bf16[16,16,128]{2,1,0:T(8,128)(2,1)S(1)}, bf16[16,16,128]{2,1,0:T(8,128)(2,1)}, u32[]{:S(2)}) copy-start(bf16[16,16,128]{2,1,0:T(8,128)(2,1)} %copy-done.16) | copy-start | bytes 196612
  181.9 12.6 %copy-start.19 = (bf16[1,1,128,256]{3,2,1,0:T(8,128)(2,1)S(1)}, bf16[1,1,128,256]{3,2,1,0:T(8,128)(2,1)}, u32[]{:S(2)}) copy-start(bf16[1,1,128,256]{3,2,1,0:T(8,128)(2,1)} %fusion.25) | copy-start | bytes 196612
  181.9 12.6 %copy-start.20 = (bf16[1,1,128,256]{3,2,1,0:T(8,128)(2,1)S(1)}, bf16[1,1,128,256]{3,2,1,0:T(8,128)(2,1)}, u32[]{:S(2)}) copy-start(bf16[1,1,128,256]{3,2,1,0:T(8,128)(2,1)} %fusion.24) | copy-start | bytes 196612
  181.9 12.6 %copy-start.21 = (bf16[1,1,128,256]{3,2,1,0:T(8,128)(2,1)S(1)}, bf16[1,1,128,256]{3,2,1,0:T(8,128)(2,1)}, u32[]{:S(2)}) copy-start(bf16[1,1,128,256]{3,2,1,0:T(8,128)(2,1)} %fusion.23) | copy-start | bytes 196612
  182.0 12.6 %copy-start.22 = (bf16[1,1,128,256]{3,2,1,0:T(8,128)(2,1)S(1)}, bf16[1,1,128,256]{3,2,1,0:T(8,128)(2,1)}, u32[]{:S(2)}) copy-start(bf16[1,1,128,256]{3,2,1,0:T(8,128)(2,1)} %fusion.22) | copy-start | bytes 196612
  182.0 12.6 %copy-start.23 = (bf16[1,1,128,256]{3,2,1,0:T(8,128)(2,1)S(1)}, bf16[1,1,128,256]{3,2,1,0:T(8,128)(2,1)}, u32[]{:S(2)}) copy-start(bf16[1,1,128,256]{3,2,1,0:T(8,128)(2,1)} %fusion.21) | copy-start | bytes 196612
  182.0 12.6 %copy-start.24 = (bf16[1,1,128,256]{3,2,1,0:T(8,128)(2,1)S(1)}, bf16[1,1,128,256]{3,2,1,0:T(8,128)(2,1)}, u32[]{:S(2)}) copy-start(bf16[1,1,128,256]{3,2,1,0:T(8,128)(2,1)} %fusion.20) | copy-start | bytes 196612
  182.7 13.1 %collective-permute-start.4 = (bf16[16,48,128]{2,1,0:T(8,128)(2,1)}, bf16[16,48,128]{2,1,0:T(8,128)(2,1)}, u32[]{:S(2)}, u32[]{:S(2)}) collective-permute-start(bf16[16,48,128]{2,1,0:T(8,128)(2,1)} %get-tuple-element.110), channel_id=1, source_target_pairs={{0,1},{1,2},{2,3},{3,4},{4,5},{5,6},{6,7},{8,9},{9,10},{10,11},{11... | collective-permute-start | bytes 589832 | tf_op jit(solution)/shard_map/ppermute | solution.py:13
  191.2 16.4 %collective-permute-start.5 = (bf16[16,48,128]{2,1,0:T(8,128)(2,1)S(1)}, bf16[16,48,128]{2,1,0:T(8,128)(2,1)}, u32[]{:S(2)}, u32[]{:S(2)}) collective-permute-start(bf16[16,48,128]{2,1,0:T(8,128)(2,1)S(1)} %get-tuple-element.111), channel_id=1, source_target_pairs={{1,0},{2,1},{3,2},{4,3},{5,4},{6,5},{7,6},{9,8},{10,9},{11,10},{12... | collective-permute-start | bytes 589832 | tf_op jit(solution)/shard_map/ppermute | solution.py:13
  208.7 21.2 %collective-permute-start.6 = (bf16[16,16,128]{2,1,0:T(8,128)(2,1)S(1)}, bf16[16,16,128]{2,1,0:T(8,128)(2,1)S(1)}, u32[]{:S(2)}, u32[]{:S(2)}) collective-permute-start(bf16[16,16,128]{2,1,0:T(8,128)(2,1)S(1)} %get-tuple-element.128), channel_id=1, source_target_pairs={{0,8},{8,16},{16,24},{24,32},{32,40},{40,48},{48,56},{56,64},{64,7... | collective-permute-start | bytes 196616 | tf_op jit(solution)/shard_map/ppermute | solution.py:13
  221.3 8.7 %collective-permute-start.7 = (bf16[16,16,128]{2,1,0:T(8,128)(2,1)S(1)}, bf16[16,16,128]{2,1,0:T(8,128)(2,1)S(1)}, u32[]{:S(2)}, u32[]{:S(2)}) collective-permute-start(bf16[16,16,128]{2,1,0:T(8,128)(2,1)S(1)} %get-tuple-element.129), channel_id=1, source_target_pairs={{8,0},{16,8},{24,16},{32,24},{40,32},{48,40},{56,48},{64,56},{72,6... | collective-permute-start | bytes 196616 | tf_op jit(solution)/shard_map/ppermute | solution.py:13
  224.3 6.3 %collective-permute-start.14 = (bf16[16,16,128]{2,1,0:T(8,128)(2,1)S(1)}, bf16[16,16,128]{2,1,0:T(8,128)(2,1)S(1)}, u32[]{:S(2)}, u32[]{:S(2)}) collective-permute-start(bf16[16,16,128]{2,1,0:T(8,128)(2,1)S(1)} %get-tuple-element.126), channel_id=1, source_target_pairs={{0,8},{8,16},{16,24},{24,32},{32,40},{40,48},{48,56},{56,64},{64,7... | collective-permute-start | bytes 196616 | tf_op jit(solution)/shard_map/ppermute | solution.py:13
  228.0 6.0 %collective-permute-start.15 = (bf16[16,16,128]{2,1,0:T(8,128)(2,1)S(1)}, bf16[16,16,128]{2,1,0:T(8,128)(2,1)S(1)}, u32[]{:S(2)}, u32[]{:S(2)}) collective-permute-start(bf16[16,16,128]{2,1,0:T(8,128)(2,1)S(1)} %get-tuple-element.127), channel_id=1, source_target_pairs={{8,0},{16,8},{24,16},{32,24},{40,32},{48,40},{56,48},{64,56},{72,6... | collective-permute-start | bytes 196616 | tf_op jit(solution)/shard_map/ppermute | solution.py:13
  (29 other events, 117.2 us)
Sparse Core Ops, SparseCore 0:
  195.9 291.1 all-reduce.44
where the time goes:
time: 502 us; the launch traced here: 499 us
  waiting for transfers between devices  273 us (54%)
  starting transfers between devices  71.1 us (14%)
  local copies, waits for them, and re-layouts  70.1 us (14%)
  matrix products  37.5 us (7%)
  between operations  30.1 us (6%)
  other arithmetic  17.1 us (3%)
    psum x1, waiting for transfers between devices, per_device(): lax.psum((d_first.astype(jnp.float32), d_down.astype(jnp.float32), d_up.a...  252 us
    unnamed x94, local copies, waits for them, and re-layouts  37.2 us
    ppermute x8, starting transfers between devices, passed_along(): return lax.ppermute(block, axis, route)  35.3 us
    ppermute x4, starting transfers between devices, extended(): before = lax.ppermute(last, axis, up)  28.4 us
    ppermute x8, waiting for transfers between devices, passed_along(): return lax.ppermute(block, axis, route)  15.2 us
    pad x3, local copies, waits for them, and re-layouts, conv_down(): padded = jnp.pad(inputs, ((1, 1), (1, 1), (0, 0)))  14.1 us
    dot_general x27, matrix products, conv_down(): jnp.dot(window, kernel[row_tap, col_tap], preferred_element_type=jnp.floa...  12.5 us
    dot_general x27, matrix products, conv_same(): jnp.dot(window, kernel[row_tap, col_tap], preferred_element_type=jnp.floa...  10.1 us
  transfers between devices with their start and end apart: 17, of which 4 were waited for; matrix products, arithmetic and copies ran while one was open for 7% of the time, Pallas kernels for 0%

commit v1 on v0

--- a/solution.py
+++ b/solution.py
@@ -169,8 +169,11 @@
     )
     field_grad = return_margins(d_canvas, tile_h, tile_w, edge)
     g_first, g_down, g_up = lax.psum(
-        (d_first.astype(jnp.float32), d_down.astype(jnp.float32), d_up.astype(jnp.float32)),
-        ("col", "row"),
+        lax.psum(
+            (d_first.astype(jnp.float32), d_down.astype(jnp.float32), d_up.astype(jnp.float32)),
+            "col",
+        ),
+        "row",
     )
     scale = 1.0 / math.sqrt(tile_h * rows_n * tile_w * cols_n)
     return (blended, field_grad, g_first * scale, g_down * scale, g_up * scale)

time: 502 us -> 953 us (1.90)
  the two profiles are of different devices: /device:TPU:17 before, /device:TPU:129 now
where the time goes in v1:
time: 953 us; the launch traced here: 951 us
  waiting for transfers between devices  731 us (77%)
  starting transfers between devices  85.4 us (9%)
  local copies, waits for them, and re-layouts  54.5 us (6%)
  matrix products  33.8 us (4%)
  between operations  29.6 us (3%)
  other arithmetic  16.2 us (2%)
    psum x1, waiting for transfers between devices, per_device(): lax.psum((d_first.astype(jnp.float32), d_down.astype(jnp.float32), d_up.a...  536 us
    psum x1, waiting for transfers between devices, per_device(): lax.psum(lax.psum((d_first.astype(jnp.float32), d_down.astype(jnp.float32...  162 us
    ppermute x8, starting transfers between devices, passed_along(): return lax.ppermute(block, axis, route)  54.7 us
    unnamed x82, local copies, waits for them, and re-layouts  31.7 us
    ppermute x8, waiting for transfers between devices, passed_along(): return lax.ppermute(block, axis, route)  26 us
    ppermute x4, starting transfers between devices, extended(): before = lax.ppermute(last, axis, up)  24 us
  transfers between devices with their start and end apart: 18, of which 6 were waited for; matrix products, arithmetic and copies ran while one was open for 3% of the time, Pallas kernels for 0%

profile of v1, /device:TPU:129, one launch (start us, length us, event | category | flops | bytes accessed | tf_op | source)
XLA Modules:
  0.0 950.7 jit_solution(1196048956024625136)
XLA Ops:
  7.2 8.8 collective-permute-start
  16.1 1.3 collective-permute-start.1
  42.9 3.9 collective-permute-start.2
  46.8 1.9 collective-permute-start.3
  48.9 8.1 collective-permute-start.8
  57.0 1.3 collective-permute-start.9
  60.9 6.9 collective-permute-done.9
  68.5 3.1 collective-permute-start.10
  71.7 1.9 collective-permute-start.11
  84.3 2.3 convert_multiply_fusion.2
  102.9 5.6 pad.345
  108.5 8.5 pad.348
  117.0 8.4 pad.346
  125.4 5.6 pad.347
  131.0 5.6 pad.214
  136.6 5.6 pad.215
  143.3 1.8 fusion.52
  153.6 535.7 %all-reduce.47.cloned.1.call-done = (f32[3,3,128,128]{3,2,1,0:T(8,128)}, f32[3,3,128,256]{3,2,1,0:T(8,128)}, f32[2,2,256,128]{3,2,1,0:T(8,128)}) async-done(((f32[3,3,128,128]{3,2,1,0:T(8,128)}, f32[3,3,128,256]{3,2,1,0:T(8,128)}, f32[2,2,256,128]{3,2,1,0:T(8,128)}), (f32[3,3,128,128]{3,2,1,0:T(8,128)}, f32[3,3,128,256]{3,2,1,0:T(8,128)}, f32[2,2,256,128]{3,2,1,0:T(8,128)})) %all-reduce.47.cloned.1.call-update) | async-done | bytes 2293776 | tf_op jit(solution)/shard_map/psum | solution.py:172
  691.5 1.3 dynamic_update_slice.7
  692.9 1.3 dynamic_update_slice.6
  694.3 6.4 collective-permute-start.4
  700.7 1.3 collective-permute-start.5
  702.0 7.9 collective-permute-start.12
  710.0 1.3 collective-permute-start.13
  711.3 8.1 collective-permute-done.5
  719.5 1.9 collective-permute-start.6
  721.4 17.8 %collective-permute-start.7 = (bf16[16,16,128]{2,1,0:T(8,128)(2,1)S(1)}, bf16[16,16,128]{2,1,0:T(8,128)(2,1)S(1)}, u32[]{:S(2)}, u32[]{:S(2)}) collective-permute-start(bf16[16,16,128]{2,1,0:T(8,128)(2,1)S(1)} %get-tuple-element.132), channel_id=1, source_target_pairs={{8,0},{16,8},{24,16},{32,24},{40,32},{48,40},{56,48},{64,56},{72,6... | collective-permute-start | bytes 196616 | tf_op jit(solution)/shard_map/ppermute | solution.py:13
  739.3 17.8 %collective-permute-done.13 = bf16[16,48,128]{2,1,0:T(8,128)(2,1)S(1)} collective-permute-done((bf16[16,48,128]{2,1,0:T(8,128)(2,1)S(1)}, bf16[16,48,128]{2,1,0:T(8,128)(2,1)S(1)}, u32[]{:S(2)}, u32[]{:S(2)}) %collective-permute-start.13) | collective-permute-done | bytes 196640 | tf_op jit(solution)/shard_map/ppermute | solution.py:13
  757.1 1.9 collective-permute-start.14
  759.1 16.2 %collective-permute-start.15 = (bf16[16,16,128]{2,1,0:T(8,128)(2,1)S(1)}, bf16[16,16,128]{2,1,0:T(8,128)(2,1)S(1)}, u32[]{:S(2)}, u32[]{:S(2)}) collective-permute-start(bf16[16,16,128]{2,1,0:T(8,128)(2,1)S(1)} %get-tuple-element.130), channel_id=1, source_target_pairs={{8,0},{16,8},{24,16},{32,24},{40,32},{48,40},{56,48},{64,56},{72,6... | collective-permute-start | bytes 196616 | tf_op jit(solution)/shard_map/ppermute | solution.py:13
  776.8 162.5 %all-reduce.49.cloned.1.call-done = (f32[3,3,128,128]{3,2,1,0:T(8,128)}, f32[3,3,128,256]{3,2,1,0:T(8,128)}, f32[2,2,256,128]{3,2,1,0:T(8,128)}) async-done(((f32[3,3,128,128]{3,2,1,0:T(8,128)}, f32[3,3,128,256]{3,2,1,0:T(8,128)}, f32[2,2,256,128]{3,2,1,0:T(8,128)}), (f32[3,3,128,128]{3,2,1,0:T(8,128)}, f32[3,3,128,256]{3,2,1,0:T(8,128)}, f32[2,2,256,128]{3,2,1,0:T(8,128)})) %all-reduce.49.cloned.1.call-update) | async-done | bytes 2293776 | tf_op jit(solution)/shard_map/psum | solution.py:171
  939.3 2.4 broadcast_multiply_fusion
  (251 shorter events, 56.6 us)
Async XLA Ops:
  7.2 35.6 %copy-start.35 = (bf16[16,16,128]{2,1,0:T(8,128)(2,1)S(1)}, bf16[16,16,128]{2,1,0:T(8,128)(2,1)}, u32[]{:S(2)}) copy-start(bf16[16,16,128]{2,1,0:T(8,128)(2,1)} %param.23) | copy-start | bytes 196612
  7.2 53.7 %copy-start.37 = (s32[32,32]{1,0:T(8,128)S(1)}, s32[32,32]{1,0:T(8,128)}, u32[]{:S(2)}) copy-start(s32[32,32]{1,0:T(8,128)} %param.29) | copy-start | bytes 12292
  7.2 41.6 %copy-start.36 = (bf16[16,16,128]{2,1,0:T(8,128)(2,1)S(1)}, bf16[16,16,128]{2,1,0:T(8,128)(2,1)}, u32[]{:S(2)}) copy-start(bf16[16,16,128]{2,1,0:T(8,128)(2,1)} %param.24) | copy-start | bytes 196612
  7.2 682.2 %all-reduce.47.cloned.1.call-start = ((), (), s32[]{:S(2)}) async-start(), calls=%async_computation | async-start | bytes 4587520 | tf_op jit(solution)/shard_map/psum | solution.py:172
  7.2 35.5 %collective-permute-start = (bf16[16,16,128]{2,1,0:T(8,128)(2,1)}, bf16[16,16,128]{2,1,0:T(8,128)(2,1)S(1)}, u32[]{:S(2)}, u32[]{:S(2)}) collective-permute-start(bf16[16,16,128]{2,1,0:T(8,128)(2,1)} %param.23), channel_id=1, source_target_pairs={{0,1},{1,2},{2,3},{3,4},{4,5},{5,6},{6,7},{8,9},{9,10},{10,11},{11... | collective-permute-start | bytes 196616 | tf_op jit(solution)/shard_map/ppermute | solution.py:23
  16.1 26.8 %collective-permute-start.1 = (bf16[16,16,128]{2,1,0:T(8,128)(2,1)}, bf16[16,16,128]{2,1,0:T(8,128)(2,1)S(1)}, u32[]{:S(2)}, u32[]{:S(2)}) collective-permute-start(bf16[16,16,128]{2,1,0:T(8,128)(2,1)} %param.23), channel_id=1, source_target_pairs={{1,0},{2,1},{3,2},{4,3},{5,4},{6,5},{7,6},{9,8},{10,9},{11,10},{12... | collective-permute-start | bytes 196616 | tf_op jit(solution)/shard_map/ppermute | solution.py:24
  42.9 30.8 %collective-permute-start.2 = (bf16[48,16,128]{2,1,0:T(8,128)(2,1)S(1)}, bf16[48,16,128]{2,1,0:T(8,128)(2,1)S(1)}, u32[]{:S(2)}, u32[]{:S(2)}) collective-permute-start(bf16[48,16,128]{2,1,0:T(8,128)(2,1)S(1)} %constant_dynamic-update-slice_fusion), channel_id=1, source_target_pairs={{0,8},{8,16},{16,24},{24,32},{32,40},{40,48},{48,56},{56,64},{64,7... | collective-permute-start | bytes 589832 | tf_op jit(solution)/shard_map/ppermute | solution.py:23
  46.8 26.8 %collective-permute-start.3 = (bf16[48,16,128]{2,1,0:T(8,128)(2,1)S(1)}, bf16[48,16,128]{2,1,0:T(8,128)(2,1)S(1)}, u32[]{:S(2)}, u32[]{:S(2)}) collective-permute-start(bf16[48,16,128]{2,1,0:T(8,128)(2,1)S(1)} %constant_dynamic-update-slice_fusion), channel_id=1, source_target_pairs={{8,0},{16,8},{24,16},{32,24},{40,32},{48,40},{56,48},{64,56},{72,6... | collective-permute-start | bytes 589832 | tf_op jit(solution)/shard_map/ppermute | solution.py:24
  48.9 12.0 %collective-permute-start.8 = (bf16[16,16,128]{2,1,0:T(8,128)(2,1)S(1)}, bf16[16,16,128]{2,1,0:T(8,128)(2,1)S(1)}, u32[]{:S(2)}, u32[]{:S(2)}) collective-permute-start(bf16[16,16,128]{2,1,0:T(8,128)(2,1)S(1)} %divide_convert_fusion), channel_id=1, source_target_pairs={{0,1},{1,2},{2,3},{3,4},{4,5},{5,6},{6,7},{8,9},{9,10},{10,11},{11... | collective-permute-start | bytes 196616 | tf_op jit(solution)/shard_map/ppermute | solution.py:23
  57.0 10.8 %collective-permute-start.9 = (bf16[16,16,128]{2,1,0:T(8,128)(2,1)S(1)}, bf16[16,16,128]{2,1,0:T(8,128)(2,1)S(1)}, u32[]{:S(2)}, u32[]{:S(2)}) collective-permute-start(bf16[16,16,128]{2,1,0:T(8,128)(2,1)S(1)} %divide_convert_fusion), channel_id=1, source_target_pairs={{1,0},{2,1},{3,2},{4,3},{5,4},{6,5},{7,6},{9,8},{10,9},{11,10},{12... | collective-permute-start | bytes 196616 | tf_op jit(solution)/shard_map/ppermute | solution.py:24
  60.9 13.3 %copy-start.28 = (bf16[16,16,128]{2,1,0:T(8,128)(2,1)}, bf16[16,16,128]{2,1,0:T(8,128)(2,1)S(1)}, u32[]{:S(2)}) copy-start(bf16[16,16,128]{2,1,0:T(8,128)(2,1)S(1)} %collective-permute-done.8) | copy-start | bytes 196612
  67.8 6.4 copy-start.30
  68.5 15.3 %collective-permute-start.10 = (bf16[48,16,128]{2,1,0:T(8,128)(2,1)}, bf16[48,16,128]{2,1,0:T(8,128)(2,1)}, u32[]{:S(2)}, u32[]{:S(2)}) collective-permute-start(bf16[48,16,128]{2,1,0:T(8,128)(2,1)} %pad_maximum_fusion.1), channel_id=1, source_target_pairs={{0,8},{8,16},{16,24},{24,32},{32,40},{40,48},{48,56},{56,64},{64,7... | collective-permute-start | bytes 589832 | tf_op jit(solution)/shard_map/ppermute | solution.py:23
  71.7 12.2 %collective-permute-start.11 = (bf16[48,16,128]{2,1,0:T(8,128)(2,1)}, bf16[48,16,128]{2,1,0:T(8,128)(2,1)}, u32[]{:S(2)}, u32[]{:S(2)}) collective-permute-start(bf16[48,16,128]{2,1,0:T(8,128)(2,1)} %pad_maximum_fusion.1), channel_id=1, source_target_pairs={{8,0},{16,8},{24,16},{32,24},{40,32},{48,40},{56,48},{64,56},{72,6... | collective-permute-start | bytes 589832 | tf_op jit(solution)/shard_map/ppermute | solution.py:24
  76.8 3.8 copy-start
  77.4 3.7 copy-start.13
  79.4 2.1 copy-start.7
  79.8 1.9 copy-start.9
  91.1 2.5 copy-start.10
  91.1 2.7 copy-start.8
  91.9 6.0 copy-start.14
  102.9 22.5 %copy-start.34 = (bf16[256,128]{1,0:T(8,128)(2,1)S(1)}, bf16[256,128]{1,0:T(8,128)(2,1)}, u32[]{:S(2)}) copy-start(bf16[256,128]{1,0:T(8,128)(2,1)} %convolution_convert_fusion.19) | copy-start | bytes 196612
  150.9 788.5 %all-reduce.49.cloned.1.call-start = ((), (), s32[]{:S(2)}) async-start(), calls=%async_computation.1 | async-start | bytes 4587520 | tf_op jit(solution)/shard_map/psum | solution.py:171
  694.3 16.9 %collective-permute-start.4 = (bf16[16,48,128]{2,1,0:T(8,128)(2,1)S(1)}, bf16[16,48,128]{2,1,0:T(8,128)(2,1)S(1)}, u32[]{:S(2)}, u32[]{:S(2)}) collective-permute-start(bf16[16,48,128]{2,1,0:T(8,128)(2,1)S(1)} %get-tuple-element.113), channel_id=1, source_target_pairs={{0,1},{1,2},{2,3},{3,4},{4,5},{5,6},{6,7},{8,9},{9,10},{10,11},{11... | collective-permute-start | bytes 589832 | tf_op jit(solution)/shard_map/ppermute | solution.py:13
  700.7 18.7 %collective-permute-start.5 = (bf16[16,48,128]{2,1,0:T(8,128)(2,1)S(1)}, bf16[16,48,128]{2,1,0:T(8,128)(2,1)S(1)}, u32[]{:S(2)}, u32[]{:S(2)}) collective-permute-start(bf16[16,48,128]{2,1,0:T(8,128)(2,1)S(1)} %get-tuple-element.114), channel_id=1, source_target_pairs={{1,0},{2,1},{3,2},{4,3},{5,4},{6,5},{7,6},{9,8},{10,9},{11,10},{12... | collective-permute-start | bytes 589832 | tf_op jit(solution)/shard_map/ppermute | solution.py:13
  702.0 37.2 %collective-permute-start.12 = (bf16[16,48,128]{2,1,0:T(8,128)(2,1)S(1)}, bf16[16,48,128]{2,1,0:T(8,128)(2,1)S(1)}, u32[]{:S(2)}, u32[]{:S(2)}) collective-permute-start(bf16[16,48,128]{2,1,0:T(8,128)(2,1)S(1)} %get-tuple-element.111), channel_id=1, source_target_pairs={{0,1},{1,2},{2,3},{3,4},{4,5},{5,6},{6,7},{8,9},{9,10},{10,11},{11... | collective-permute-start | bytes 589832 | tf_op jit(solution)/shard_map/ppermute | solution.py:13
  710.0 47.1 %collective-permute-start.13 = (bf16[16,48,128]{2,1,0:T(8,128)(2,1)S(1)}, bf16[16,48,128]{2,1,0:T(8,128)(2,1)S(1)}, u32[]{:S(2)}, u32[]{:S(2)}) collective-permute-start(bf16[16,48,128]{2,1,0:T(8,128)(2,1)S(1)} %get-tuple-element.112), channel_id=1, source_target_pairs={{1,0},{2,1},{3,2},{4,3},{5,4},{6,5},{7,6},{9,8},{10,9},{11,10},{12... | collective-permute-start | bytes 589832 | tf_op jit(solution)/shard_map/ppermute | solution.py:13
  719.5 55.8 %collective-permute-start.6 = (bf16[16,16,128]{2,1,0:T(8,128)(2,1)S(1)}, bf16[16,16,128]{2,1,0:T(8,128)(2,1)S(1)}, u32[]{:S(2)}, u32[]{:S(2)}) collective-permute-start(bf16[16,16,128]{2,1,0:T(8,128)(2,1)S(1)} %get-tuple-element.131), channel_id=1, source_target_pairs={{0,8},{8,16},{16,24},{24,32},{32,40},{40,48},{48,56},{56,64},{64,7... | collective-permute-start | bytes 196616 | tf_op jit(solution)/shard_map/ppermute | solution.py:13
  721.4 53.9 %collective-permute-start.7 = (bf16[16,16,128]{2,1,0:T(8,128)(2,1)S(1)}, bf16[16,16,128]{2,1,0:T(8,128)(2,1)S(1)}, u32[]{:S(2)}, u32[]{:S(2)}) collective-permute-start(bf16[16,16,128]{2,1,0:T(8,128)(2,1)S(1)} %get-tuple-element.132), channel_id=1, source_target_pairs={{8,0},{16,8},{24,16},{32,24},{40,32},{48,40},{56,48},{64,56},{72,6... | collective-permute-start | bytes 196616 | tf_op jit(solution)/shard_map/ppermute | solution.py:13
  757.1 18.9 %collective-permute-start.14 = (bf16[16,16,128]{2,1,0:T(8,128)(2,1)S(1)}, bf16[16,16,128]{2,1,0:T(8,128)(2,1)S(1)}, u32[]{:S(2)}, u32[]{:S(2)}) collective-permute-start(bf16[16,16,128]{2,1,0:T(8,128)(2,1)S(1)} %get-tuple-element.129), channel_id=1, source_target_pairs={{0,8},{8,16},{16,24},{24,32},{32,40},{40,48},{48,56},{56,64},{64,7... | collective-permute-start | bytes 196616 | tf_op jit(solution)/shard_map/ppermute | solution.py:13
  759.1 17.1 %collective-permute-start.15 = (bf16[16,16,128]{2,1,0:T(8,128)(2,1)S(1)}, bf16[16,16,128]{2,1,0:T(8,128)(2,1)S(1)}, u32[]{:S(2)}, u32[]{:S(2)}) collective-permute-start(bf16[16,16,128]{2,1,0:T(8,128)(2,1)S(1)} %get-tuple-element.130), channel_id=1, source_target_pairs={{8,0},{16,8},{24,16},{32,24},{40,32},{48,40},{56,48},{64,56},{72,6... | collective-permute-start | bytes 196616 | tf_op jit(solution)/shard_map/ppermute | solution.py:13
  939.3 2.5 copy-start.6
  (24 other events, 30.9 us)
Sparse Core Ops, SparseCore 0:
  151.0 538.3 all-reduce.46
  692.9 246.3 all-reduce.48
